TPU v7x, 512 devices: a whole 4x4x16 slice. The times are simulated.
512 devices in a mesh: blk: 64 (over z, x_hi, core), sub: 8 (over y, x_lo).
Axes of the slice: x: 4 (x_hi: 2, x_lo: 2; x = x_hi * 2 + x_lo), y: 4, z: 16, core: 2. Of those that a mesh axis runs over, the one named last changes fastest.
Arguments:
- features: float32 [12, 256, 8192], P(None, 'sub', 'blk'), may hold values from -6 to 6
- inverse_diag: float32 [6, 6, 256, 8192], P(None, None, 'sub', 'blk'), may hold values from -0.12 to 1, as said below
- couplings: float32 [4, 256, 8192], P(None, 'sub', 'blk'), may hold values from 0.2 to 0.24
- mismatch: float32 [6, 256, 8192], P(None, 'sub', 'blk'), may hold values from -21 to 21
- production: float32 [6, 256, 8192], P(None, 'sub', 'blk'), may hold values from -6 to 6
- weight_in: float32 [128, 12], replicated, may hold values from -1.75 to 1.75
- bias_in: float32 [128], replicated, may hold values from -0.5 to 0.5
- weight_two: float32 [128, 128], replicated, may hold values from -0.5 to 0.5
- bias_two: float32 [128], replicated, may hold values from -0.5 to 0.5
- weight_three: float32 [128, 128], replicated, may hold values from -0.5 to 0.5
- bias_three: float32 [128], replicated, may hold values from -0.5 to 0.5
- weight_four: float32 [128, 128], replicated, may hold values from -0.5 to 0.5
- bias_four: float32 [128], replicated, may hold values from -0.5 to 0.5
- weight_out: float32 [128], replicated, may hold values from -0.5 to 0.5
Outputs:
- adjoint: float32 [6, 256, 8192], P(None, 'sub', 'blk')
- sensitivity: float32 [256, 8192], P('sub', 'blk')
- correction: float32 [256, 8192], P('sub', 'blk')
- grad_weight_in: float32 [128, 12], replicated
- grad_bias_in: float32 [128], replicated
- grad_weight_two: float32 [128, 128], replicated
- grad_bias_two: float32 [128], replicated
- grad_weight_three: float32 [128, 128], replicated
- grad_bias_three: float32 [128], replicated
- grad_weight_four: float32 [128, 128], replicated
- grad_bias_four: float32 [128], replicated
- grad_weight_out: float32 [128], replicated
Inputs may be any that keep to these rules, and one draw needn't show every extreme that they name: `inverse_diag`: a cell's 6 by 6 block with diagonal entries between 0.7 and 1.0 and off-diagonal entries of magnitude at most 0.12.
All inputs are finite; a program needn't handle non-finite values.
Results may differ from a plain program's by a relative error of at most 0.0003.
Values sent between devices are 32-bit elements; how exact they have to be, the bound alone decides.
No kernel may reach another device: no remote copies, remote signals or barrier semaphores. Data moves between devices by JAX's collectives and lax.ppermute only.
A program may use at most 64 MiB of HBM per device.

v0:
```python
import jax
import jax.numpy as jnp
from jax import lax
from jax.sharding import PartitionSpec as P

SWEEPS = 8
EPS = 1e-06
HIGH = lax.Precision.HIGHEST


def padded_2(value, sides, width, wrap):
    for axis, dim in sides:
        devices, length = (lax.axis_size(axis), value.shape[dim])
        up = [(i, (i + 1) % devices) for i in range(devices if wrap else devices - 1)]
        down = [(j, i) for i, j in up]
        last = lax.slice_in_dim(value, length - width, length, axis=dim)
        initial = lax.slice_in_dim(value, 0, width, axis=dim)
        before = lax.ppermute(last, axis, up)
        after = lax.ppermute(initial, axis, down)
        value = jnp.concatenate([before, value, after], axis=dim)
    return value


def sweep_padded(padded, inverse_diag, couplings, mismatch):
    upper_side = padded[:, :-2, 1:-1]
    lower_side = padded[:, 2:, 1:-1]
    pitch_low = padded[:, 1:-1, :-2]
    pitch_high = padded[:, 1:-1, 2:]
    rhs = mismatch + couplings[0] * upper_side + couplings[1] * lower_side
    rhs = rhs + couplings[2] * pitch_low + couplings[3] * pitch_high
    return jnp.sum(inverse_diag * rhs[None], axis=1)


def forward(inputs, weights):
    weight_in, bias_in, weight_two, bias_two, weight_three, bias_three, weight_four, bias_four = (
        weights
    )
    layer_one = jnp.tanh(
        jnp.einsum("ij,jc->ic", weight_in, inputs, precision=HIGH) + bias_in[:, None]
    )
    layer_two = jnp.tanh(
        jnp.einsum("ij,jc->ic", weight_two, layer_one, precision=HIGH) + bias_two[:, None]
    )
    layer_three = jnp.tanh(
        jnp.einsum("ij,jc->ic", weight_three, layer_two, precision=HIGH) + bias_three[:, None]
    )
    layer_four = jnp.tanh(
        jnp.einsum("ij,jc->ic", weight_four, layer_three, precision=HIGH) + bias_four[:, None]
    )
    return (layer_one, layer_two, layer_three, layer_four)


def top_terms(layer_four, layer_three, upstream, weight_out):
    grad_out = jnp.einsum("ic,c->i", layer_four, upstream, precision=HIGH)
    delta_four = weight_out[:, None] * upstream[None, :] * (1.0 - layer_four * layer_four)
    grad_four = jnp.einsum("ic,jc->ij", delta_four, layer_three, precision=HIGH)
    return (grad_out, grad_four, jnp.sum(delta_four, axis=1), delta_four)


def next_terms(delta_next, weight_next, layer_now, layer_prev):
    delta_now = jnp.einsum("ji,jc->ic", weight_next, delta_next, precision=HIGH) * (
        1.0 - layer_now * layer_now
    )
    grad_now = jnp.einsum("ic,jc->ij", delta_now, layer_prev, precision=HIGH)
    return (grad_now, jnp.sum(delta_now, axis=1), delta_now)


def local(
    features,
    inverse_diag,
    couplings,
    mismatch,
    production,
    weight_in,
    bias_in,
    weight_two,
    bias_two,
    weight_three,
    bias_three,
    weight_four,
    bias_four,
    weight_out,
):
    nvars, rows, cols = mismatch.shape
    adjoint = jnp.zeros((nvars, rows, cols), jnp.float32)
    for sweep_index in range(SWEEPS):
        widened = padded_2(adjoint, (("blk", 2),), 1, True)
        padded = padded_2(widened, (("sub", 1),), 1, False)
        adjoint = sweep_padded(padded, inverse_diag, couplings, mismatch)
    sensitivity = -jnp.sum(adjoint * production, axis=0)
    local_square = jnp.sum(sensitivity * sensitivity)
    inputs = features.reshape(features.shape[0], rows * cols)
    weights = (
        weight_in,
        bias_in,
        weight_two,
        bias_two,
        weight_three,
        bias_three,
        weight_four,
        bias_four,
    )
    layer_one, layer_two, layer_three, layer_four = forward(inputs, weights)
    correction = (1.0 + jnp.einsum("i,ic->c", weight_out, layer_four, precision=HIGH)).reshape(
        rows, cols
    )
    flat_sens = sensitivity.reshape(rows * cols)
    total_square = lax.psum(local_square, ("blk", "sub"))
    norm_value = jnp.sqrt(total_square + EPS)
    upstream = flat_sens / norm_value
    grad_out, grad_four, gb_four, delta_four = top_terms(
        layer_four, layer_three, upstream, weight_out
    )
    grad_out, grad_four, gb_four = lax.psum((grad_out, grad_four, gb_four), ("blk", "sub"))
    grad_three, gb_three, delta_three = next_terms(delta_four, weight_four, layer_three, layer_two)
    grad_three, gb_three = lax.psum((grad_three, gb_three), ("blk", "sub"))
    grad_two, gb_two, delta_two = next_terms(delta_three, weight_three, layer_two, layer_one)
    grad_two, gb_two = lax.psum((grad_two, gb_two), ("blk", "sub"))
    grad_one, gb_one, delta_one = next_terms(delta_two, weight_two, layer_one, inputs)
    grad_one, gb_one = lax.psum((grad_one, gb_one), ("blk", "sub"))
    results = (
        grad_one,
        gb_one,
        grad_two,
        gb_two,
        grad_three,
        gb_three,
        grad_four,
        gb_four,
        grad_out,
    )
    return (
        adjoint,
        sensitivity,
        correction,
        results[0],
        results[1],
        results[2],
        results[3],
        results[4],
        results[5],
        results[6],
        results[7],
        results[8],
    )


def solution(mesh):
    placed = (
        P(None, "sub", "blk"),
        P(None, None, "sub", "blk"),
        P(None, "sub", "blk"),
        P(None, "sub", "blk"),
        P(None, "sub", "blk"),
        P(),
        P(),
        P(),
        P(),
        P(),
        P(),
        P(),
        P(),
        P(),
    )
    return jax.shard_map(
        local,
        mesh=mesh,
        in_specs=placed,
        out_specs=(
            P(None, "sub", "blk"),
            P("sub", "blk"),
            P("sub", "blk"),
            P(),
            P(),
            P(),
            P(),
            P(),
            P(),
            P(),
            P(),
            P(),
        ),
        check_vma=False,
    )
```

profile of v0, /device:TPU:1, one launch (start us, length us, event | category | flops | bytes accessed | tf_op | source)
XLA Modules:
  0.0 789.4 jit_solution(17911993634000659095)
XLA Ops:
  7.3 8.9 %collective-permute-start.1 = (f32[6,32,1]{2,1,0:T(8,128)S(1)}, f32[6,32,1]{2,1,0:T(8,128)S(1)}, u32[]{:S(2)}, u32[]{:S(2)}) collective-permute-start(f32[6,32,1]{2,1,0:T(8,128)S(1)} %broadcast.37), channel_id=1, source_target_pairs={{8,0},{16,8},{24,16},{32,24},{40,32},{48,40},{56,48},{64,56},{72,6... | collective-permute-start | bytes 2312 | tf_op jit(solution)/shard_map/ppermute | solution.py:19
  16.2 1.9 collective-permute-start
  18.1 6.8 collective-permute-done
  25.0 2.2 collective-permute-start.2
  29.4 3.0 collective-permute-done.3
  34.7 1.9 collective-permute-start.4
  36.6 9.9 %collective-permute-start.5 = (f32[6,32,1]{2,1,0:T(8,128)S(1)}, f32[6,32,1]{2,1,0:T(8,128)S(1)}, u32[]{:S(2)}, u32[]{:S(2)}) collective-permute-start(f32[6,32,1]{2,1,0:T(8,128)S(1)} %get-tuple-element.52), channel_id=1, source_target_pairs={{8,0},{16,8},{24,16},{32,24},{40,32},{48,40},{56,48},{64,56},{72,6... | collective-permute-start | bytes 2312 | tf_op jit(solution)/shard_map/ppermute | solution.py:19
  47.5 4.5 collective-permute-start.6
  53.4 3.1 collective-permute-done.7
  56.8 1.9 collective-permute-start.8
  58.8 10.0 %collective-permute-start.9 = (f32[6,32,1]{2,1,0:T(8,128)S(1)}, f32[6,32,1]{2,1,0:T(8,128)S(1)}, u32[]{:S(2)}, u32[]{:S(2)}) collective-permute-start(f32[6,32,1]{2,1,0:T(8,128)S(1)} %get-tuple-element.50), channel_id=1, source_target_pairs={{8,0},{16,8},{24,16},{32,24},{40,32},{48,40},{56,48},{64,56},{72,6... | collective-permute-start | bytes 2312 | tf_op jit(solution)/shard_map/ppermute | solution.py:19
  69.8 2.7 collective-permute-start.10
  73.7 3.3 collective-permute-done.11
  77.4 1.9 collective-permute-start.12
  79.4 9.7 %collective-permute-start.13 = (f32[6,32,1]{2,1,0:T(8,128)S(1)}, f32[6,32,1]{2,1,0:T(8,128)S(1)}, u32[]{:S(2)}, u32[]{:S(2)}) collective-permute-start(f32[6,32,1]{2,1,0:T(8,128)S(1)} %get-tuple-element.48), channel_id=1, source_target_pairs={{8,0},{16,8},{24,16},{32,24},{40,32},{48,40},{56,48},{64,56},{72,6... | collective-permute-start | bytes 2312 | tf_op jit(solution)/shard_map/ppermute | solution.py:19
  90.1 4.5 collective-permute-start.14
  95.9 3.1 collective-permute-done.15
  99.4 1.9 collective-permute-start.16
  101.3 10.0 %collective-permute-start.17 = (f32[6,32,1]{2,1,0:T(8,128)S(1)}, f32[6,32,1]{2,1,0:T(8,128)S(1)}, u32[]{:S(2)}, u32[]{:S(2)}) collective-permute-start(f32[6,32,1]{2,1,0:T(8,128)S(1)} %get-tuple-element.46), channel_id=1, source_target_pairs={{8,0},{16,8},{24,16},{32,24},{40,32},{48,40},{56,48},{64,56},{72,6... | collective-permute-start | bytes 2312 | tf_op jit(solution)/shard_map/ppermute | solution.py:19
  112.3 2.7 collective-permute-start.18
  116.3 3.2 collective-permute-done.19
  119.8 1.9 collective-permute-start.20
  121.8 10.0 %collective-permute-start.21 = (f32[6,32,1]{2,1,0:T(8,128)S(1)}, f32[6,32,1]{2,1,0:T(8,128)S(1)}, u32[]{:S(2)}, u32[]{:S(2)}) collective-permute-start(f32[6,32,1]{2,1,0:T(8,128)S(1)} %get-tuple-element.44), channel_id=1, source_target_pairs={{8,0},{16,8},{24,16},{32,24},{40,32},{48,40},{56,48},{64,56},{72,6... | collective-permute-start | bytes 2312 | tf_op jit(solution)/shard_map/ppermute | solution.py:19
  132.8 4.2 collective-permute-start.22
  138.3 3.1 collective-permute-done.23
  141.8 1.9 collective-permute-start.24
  143.7 10.0 %collective-permute-start.25 = (f32[6,32,1]{2,1,0:T(8,128)S(1)}, f32[6,32,1]{2,1,0:T(8,128)S(1)}, u32[]{:S(2)}, u32[]{:S(2)}) collective-permute-start(f32[6,32,1]{2,1,0:T(8,128)S(1)} %get-tuple-element.42), channel_id=1, source_target_pairs={{8,0},{16,8},{24,16},{32,24},{40,32},{48,40},{56,48},{64,56},{72,6... | collective-permute-start | bytes 2312 | tf_op jit(solution)/shard_map/ppermute | solution.py:19
  154.7 2.8 collective-permute-start.26
  159.1 2.8 collective-permute-done.27
  162.3 1.9 collective-permute-start.28
  164.2 10.0 %collective-permute-start.29 = (f32[6,32,1]{2,1,0:T(8,128)S(1)}, f32[6,32,1]{2,1,0:T(8,128)S(1)}, u32[]{:S(2)}, u32[]{:S(2)}) collective-permute-start(f32[6,32,1]{2,1,0:T(8,128)S(1)} %get-tuple-element.40), channel_id=1, source_target_pairs={{8,0},{16,8},{24,16},{32,24},{40,32},{48,40},{56,48},{64,56},{72,6... | collective-permute-start | bytes 2312 | tf_op jit(solution)/shard_map/ppermute | solution.py:19
  174.2 1.9 fusion.5
  176.2 2.5 collective-permute-start.30
  178.8 1.9 collective-permute-start.31
  180.7 3.4 fusion.4
  185.5 3.2 fusion.3
  188.7 108.6 %psum.70 = f32[]{:T(128)} all-reduce(f32[]{:T(128)} %multiply_reduce_fusion.9), channel_id=1, replica_groups=mesh['blk'=64,'sub'=8] {'blk','sub'}, use_global_device_ids=true, to_apply=%region_10.0 | all-reduce | flops 1 | bytes 8 | tf_op jit(solution)/shard_map/psum | solution.py:108
  298.6 4.0 fusion.6
  304.3 3.1 fusion.7
  307.4 3.6 fusion.91
  311.0 4.4 fusion.94
  315.4 1.9 fusion.90
  318.6 4.2 fusion.93
  322.8 4.5 fusion.89
  328.0 1.7 fusion.92
  329.7 1.7 convolution_bitcast_fusion.1
  331.4 99.6 %all-reduce.2 = (f32[128,12]{0,1:T(8,128)}, f32[128]{0:T(128)}, f32[128]{0:T(128)}, f32[128]{0:T(128)}, f32[128]{0:T(128)}, /*index=5*/f32[128]{0:T(128)}) all-reduce(f32[128,12]{0,1:T(8,128)S(1)} %fusion.92, f32[128]{0:T(128)S(1)} %get-tuple-element.57, ...), channel_id=1, replica_groups=mesh['blk'=64,'sub'=8] {'blk','sub'}, use_global_device_ids=true, to_apply=%region_11.0 | all-reduce | flops 2176 | bytes 17408 | tf_op jit(solution)/shard_map/psum | solution.py:120
  431.1 346.9 %all-reduce.6.cloned.1.call-done = (f32[128,128]{1,0:T(8,128)}, f32[128,128]{1,0:T(8,128)}, f32[128,128]{1,0:T(8,128)}) async-done(((f32[128,128]{1,0:T(8,128)}, f32[128,128]{1,0:T(8,128)}, f32[128,128]{1,0:T(8,128)}), (f32[128,128]{1,0:T(8,128)}, f32[128,128]{1,0:T(8,128)}, f32[128,128]{1,0:T(8,128)})) %all-reduce.6.cloned.1.call-update) | async-done | bytes 196624 | tf_op jit(solution)/shard_map/psum | solution.py:118
  (117 shorter events, 30.7 us)
Async XLA Ops:
  7.2 291.5 %copy-start = (f32[128,128]{1,0:T(8,128)S(1)}, f32[128,128]{1,0:T(8,128)}, u32[]{:S(2)}) copy-start(f32[128,128]{1,0:T(8,128)} %param.25) | copy-start | bytes 196612
  7.2 49.3 %copy-start.8 = (f32[6,32,128]{2,1,0:T(8,128)S(1)}, f32[6,32,128]{2,1,0:T(8,128)}, u32[]{:S(2)}) copy-start(f32[6,32,128]{2,1,0:T(8,128)} %param.17) | copy-start | bytes 294916
  7.2 49.5 %copy-start.1 = (f32[6,6,32,128]{3,2,1,0:T(8,128)S(1)}, f32[6,6,32,128]{3,2,1,0:T(8,128)}, u32[]{:S(2)}) copy-start(f32[6,6,32,128]{3,2,1,0:T(8,128)} %param.15) | copy-start | bytes 1769476
  7.2 770.7 %all-reduce.6.cloned.1.call-start = ((), (), s32[]{:S(2)}) async-start(), calls=%async_computation | async-start | bytes 393216 | tf_op jit(solution)/shard_map/psum | solution.py:118
  7.3 10.9 %collective-permute-start.1 = (f32[6,32,1]{2,1,0:T(8,128)S(1)}, f32[6,32,1]{2,1,0:T(8,128)S(1)}, u32[]{:S(2)}, u32[]{:S(2)}) collective-permute-start(f32[6,32,1]{2,1,0:T(8,128)S(1)} %broadcast.37), channel_id=1, source_target_pairs={{8,0},{16,8},{24,16},{32,24},{40,32},{48,40},{56,48},{64,56},{72,6... | collective-permute-start | bytes 2312 | tf_op jit(solution)/shard_map/ppermute | solution.py:19
  16.2 8.7 %collective-permute-start = (f32[6,32,1]{2,1,0:T(8,128)S(1)}, f32[6,32,1]{2,1,0:T(8,128)S(1)}, u32[]{:S(2)}, u32[]{:S(2)}) collective-permute-start(f32[6,32,1]{2,1,0:T(8,128)S(1)} %broadcast.37), channel_id=1, source_target_pairs={{0,8},{8,16},{16,24},{24,32},{32,40},{40,48},{48,56},{56,64},{64,7... | collective-permute-start | bytes 2312 | tf_op jit(solution)/shard_map/ppermute | solution.py:18
  25.0 4.3 collective-permute-start.2
  27.3 5.1 collective-permute-start.3
  34.7 11.8 %collective-permute-start.4 = (f32[6,32,1]{2,1,0:T(8,128)S(1)}, f32[6,32,1]{2,1,0:T(8,128)S(1)}, u32[]{:S(2)}, u32[]{:S(2)}) collective-permute-start(f32[6,32,1]{2,1,0:T(8,128)S(1)} %get-tuple-element.51), channel_id=1, source_target_pairs={{0,8},{8,16},{16,24},{24,32},{32,40},{40,48},{48,56},{56,64},{64,7... | collective-permute-start | bytes 2312 | tf_op jit(solution)/shard_map/ppermute | solution.py:18
  36.6 10.8 %collective-permute-start.5 = (f32[6,32,1]{2,1,0:T(8,128)S(1)}, f32[6,32,1]{2,1,0:T(8,128)S(1)}, u32[]{:S(2)}, u32[]{:S(2)}) collective-permute-start(f32[6,32,1]{2,1,0:T(8,128)S(1)} %get-tuple-element.52), channel_id=1, source_target_pairs={{8,0},{16,8},{24,16},{32,24},{40,32},{48,40},{56,48},{64,56},{72,6... | collective-permute-start | bytes 2312 | tf_op jit(solution)/shard_map/ppermute | solution.py:19
  47.5 5.8 collective-permute-start.6
  52.1 4.4 collective-permute-start.7
  56.8 11.9 %collective-permute-start.8 = (f32[6,32,1]{2,1,0:T(8,128)S(1)}, f32[6,32,1]{2,1,0:T(8,128)S(1)}, u32[]{:S(2)}, u32[]{:S(2)}) collective-permute-start(f32[6,32,1]{2,1,0:T(8,128)S(1)} %get-tuple-element.49), channel_id=1, source_target_pairs={{0,8},{8,16},{16,24},{24,32},{32,40},{40,48},{48,56},{56,64},{64,7... | collective-permute-start | bytes 2312 | tf_op jit(solution)/shard_map/ppermute | solution.py:18
  58.8 10.9 %collective-permute-start.9 = (f32[6,32,1]{2,1,0:T(8,128)S(1)}, f32[6,32,1]{2,1,0:T(8,128)S(1)}, u32[]{:S(2)}, u32[]{:S(2)}) collective-permute-start(f32[6,32,1]{2,1,0:T(8,128)S(1)} %get-tuple-element.50), channel_id=1, source_target_pairs={{8,0},{16,8},{24,16},{32,24},{40,32},{48,40},{56,48},{64,56},{72,6... | collective-permute-start | bytes 2312 | tf_op jit(solution)/shard_map/ppermute | solution.py:19
  69.8 4.0 collective-permute-start.10
  72.4 4.7 collective-permute-start.11
  77.4 11.6 %collective-permute-start.12 = (f32[6,32,1]{2,1,0:T(8,128)S(1)}, f32[6,32,1]{2,1,0:T(8,128)S(1)}, u32[]{:S(2)}, u32[]{:S(2)}) collective-permute-start(f32[6,32,1]{2,1,0:T(8,128)S(1)} %get-tuple-element.47), channel_id=1, source_target_pairs={{0,8},{8,16},{16,24},{24,32},{32,40},{40,48},{48,56},{56,64},{64,7... | collective-permute-start | bytes 2312 | tf_op jit(solution)/shard_map/ppermute | solution.py:18
  79.4 10.6 %collective-permute-start.13 = (f32[6,32,1]{2,1,0:T(8,128)S(1)}, f32[6,32,1]{2,1,0:T(8,128)S(1)}, u32[]{:S(2)}, u32[]{:S(2)}) collective-permute-start(f32[6,32,1]{2,1,0:T(8,128)S(1)} %get-tuple-element.48), channel_id=1, source_target_pairs={{8,0},{16,8},{24,16},{32,24},{40,32},{48,40},{56,48},{64,56},{72,6... | collective-permute-start | bytes 2312 | tf_op jit(solution)/shard_map/ppermute | solution.py:19
  90.1 5.8 collective-permute-start.14
  94.6 4.4 collective-permute-start.15
  99.4 11.9 %collective-permute-start.16 = (f32[6,32,1]{2,1,0:T(8,128)S(1)}, f32[6,32,1]{2,1,0:T(8,128)S(1)}, u32[]{:S(2)}, u32[]{:S(2)}) collective-permute-start(f32[6,32,1]{2,1,0:T(8,128)S(1)} %get-tuple-element.45), channel_id=1, source_target_pairs={{0,8},{8,16},{16,24},{24,32},{32,40},{40,48},{48,56},{56,64},{64,7... | collective-permute-start | bytes 2312 | tf_op jit(solution)/shard_map/ppermute | solution.py:18
  101.3 10.9 %collective-permute-start.17 = (f32[6,32,1]{2,1,0:T(8,128)S(1)}, f32[6,32,1]{2,1,0:T(8,128)S(1)}, u32[]{:S(2)}, u32[]{:S(2)}) collective-permute-start(f32[6,32,1]{2,1,0:T(8,128)S(1)} %get-tuple-element.46), channel_id=1, source_target_pairs={{8,0},{16,8},{24,16},{32,24},{40,32},{48,40},{56,48},{64,56},{72,6... | collective-permute-start | bytes 2312 | tf_op jit(solution)/shard_map/ppermute | solution.py:19
  112.3 46.6 %copy-start.12 = (f32[12,32,128]{2,1,0:T(8,128)S(1)}, f32[12,32,128]{2,1,0:T(8,128)}, u32[]{:S(2)}) copy-start(f32[12,32,128]{2,1,0:T(8,128)} %param.14) | copy-start | bytes 589828
  112.3 4.0 collective-permute-start.18
  115.0 4.5 collective-permute-start.19
  119.8 11.9 %collective-permute-start.20 = (f32[6,32,1]{2,1,0:T(8,128)S(1)}, f32[6,32,1]{2,1,0:T(8,128)S(1)}, u32[]{:S(2)}, u32[]{:S(2)}) collective-permute-start(f32[6,32,1]{2,1,0:T(8,128)S(1)} %get-tuple-element.43), channel_id=1, source_target_pairs={{0,8},{8,16},{16,24},{24,32},{32,40},{40,48},{48,56},{56,64},{64,7... | collective-permute-start | bytes 2312 | tf_op jit(solution)/shard_map/ppermute | solution.py:18
  121.8 10.9 %collective-permute-start.21 = (f32[6,32,1]{2,1,0:T(8,128)S(1)}, f32[6,32,1]{2,1,0:T(8,128)S(1)}, u32[]{:S(2)}, u32[]{:S(2)}) collective-permute-start(f32[6,32,1]{2,1,0:T(8,128)S(1)} %get-tuple-element.44), channel_id=1, source_target_pairs={{8,0},{16,8},{24,16},{32,24},{40,32},{48,40},{56,48},{64,56},{72,6... | collective-permute-start | bytes 2312 | tf_op jit(solution)/shard_map/ppermute | solution.py:19
  132.8 5.5 collective-permute-start.22
  137.0 4.4 collective-permute-start.23
  141.6 32.6 %copy-start.14 = (f32[128,12]{0,1:T(8,128)S(1)}, f32[128,12]{0,1:T(8,128)}, u32[]{:S(2)}) copy-start(f32[128,12]{0,1:T(8,128)} %param.19) | copy-start | bytes 18436
  141.6 32.6 %copy-start.19 = (f32[128]{0:T(128)S(1)}, f32[128]{0:T(128)}, u32[]{:S(2)}) copy-start(f32[128]{0:T(128)} %param.20) | copy-start | bytes 1540
  141.8 11.9 %collective-permute-start.24 = (f32[6,32,1]{2,1,0:T(8,128)S(1)}, f32[6,32,1]{2,1,0:T(8,128)S(1)}, u32[]{:S(2)}, u32[]{:S(2)}) collective-permute-start(f32[6,32,1]{2,1,0:T(8,128)S(1)} %get-tuple-element.41), channel_id=1, source_target_pairs={{0,8},{8,16},{16,24},{24,32},{32,40},{40,48},{48,56},{56,64},{64,7... | collective-permute-start | bytes 2312 | tf_op jit(solution)/shard_map/ppermute | solution.py:18
  143.7 10.9 %collective-permute-start.25 = (f32[6,32,1]{2,1,0:T(8,128)S(1)}, f32[6,32,1]{2,1,0:T(8,128)S(1)}, u32[]{:S(2)}, u32[]{:S(2)}) collective-permute-start(f32[6,32,1]{2,1,0:T(8,128)S(1)} %get-tuple-element.42), channel_id=1, source_target_pairs={{8,0},{16,8},{24,16},{32,24},{40,32},{48,40},{56,48},{64,56},{72,6... | collective-permute-start | bytes 2312 | tf_op jit(solution)/shard_map/ppermute | solution.py:19
  154.7 4.4 collective-permute-start.26
  157.6 4.4 collective-permute-start.27
  159.1 21.7 %copy-start.11 = (f32[128,128]{1,0:T(8,128)S(1)}, f32[128,128]{1,0:T(8,128)}, u32[]{:S(2)}) copy-start(f32[128,128]{1,0:T(8,128)} %param.21) | copy-start | bytes 196612
  159.1 21.7 %copy-start.16 = (f32[128]{0:T(128)S(1)}, f32[128]{0:T(128)}, u32[]{:S(2)}) copy-start(f32[128]{0:T(128)} %param.22) | copy-start | bytes 1540
  162.3 13.8 %collective-permute-start.28 = (f32[6,32,1]{2,1,0:T(8,128)S(1)}, f32[6,32,1]{2,1,0:T(8,128)S(1)}, u32[]{:S(2)}, u32[]{:S(2)}) collective-permute-start(f32[6,32,1]{2,1,0:T(8,128)S(1)} %get-tuple-element.39), channel_id=1, source_target_pairs={{0,8},{8,16},{16,24},{24,32},{32,40},{40,48},{48,56},{56,64},{64,7... | collective-permute-start | bytes 2312 | tf_op jit(solution)/shard_map/ppermute | solution.py:18
  164.2 11.9 %collective-permute-start.29 = (f32[6,32,1]{2,1,0:T(8,128)S(1)}, f32[6,32,1]{2,1,0:T(8,128)S(1)}, u32[]{:S(2)}, u32[]{:S(2)}) collective-permute-start(f32[6,32,1]{2,1,0:T(8,128)S(1)} %get-tuple-element.40), channel_id=1, source_target_pairs={{8,0},{16,8},{24,16},{32,24},{40,32},{48,40},{56,48},{64,56},{72,6... | collective-permute-start | bytes 2312 | tf_op jit(solution)/shard_map/ppermute | solution.py:19
  176.1 8.1 %copy-start.2 = (f32[128,4096]{1,0:T(8,128)}, f32[128,4096]{1,0:T(8,128)S(1)}, u32[]{:S(2)}) copy-start(f32[128,4096]{1,0:T(8,128)S(1)} %fusion.5) | copy-start | bytes 6291460
  176.2 8.0 %collective-permute-start.30 = (f32[6,1,130]{2,1,0:T(1,128)S(1)}, f32[6,1,130]{2,1,0:T(1,128)S(1)}, u32[]{:S(2)}, u32[]{:S(2)}) collective-permute-start(f32[6,1,130]{2,1,0:T(1,128)S(1)} %get-tuple-element.23), channel_id=1, source_target_pairs={{0,1},{1,2},{2,3},{3,4},{4,5},{5,6},{6,7},{8,9},{9,10},{10,11},{11... | collective-permute-start | bytes 9368 | tf_op jit(solution)/shard_map/ppermute | solution.py:18
  178.8 5.7 copy-start.13
  178.8 6.7 copy-start.10
  178.8 6.7 copy-start.17
  178.8 5.4 collective-permute-start.31
  184.5 4.2 copy-start.9
  185.5 113.1 %copy-start.15 = (f32[128]{0:T(128)S(1)}, f32[128]{0:T(128)}, u32[]{:S(2)}) copy-start(f32[128]{0:T(128)} %param.27) | copy-start | bytes 1540
  185.5 113.1 %copy-start.18 = (f32[128]{0:T(128)S(1)}, f32[128]{0:T(128)}, u32[]{:S(2)}) copy-start(f32[128]{0:T(128)} %param.26) | copy-start | bytes 1540
  (5 other events, 11.1 us)
Sparse Core Ops, SparseCore 0:
  329.8 448.0 all-reduce.5
where the time goes:
time: 796 us; the launch traced here: 789 us
  waiting for transfers between devices  381 us (48%)
  blocking collectives  208 us (26%)
  starting transfers between devices  131 us (16%)
  matrix products  38.9 us (5%)
  between operations  15.8 us (2%)
    psum x1, waiting for transfers between devices, local(): grad_two, gb_two = lax.psum((grad_two, gb_two), ('blk', 'sub'))  347 us
    psum x1, blocking collectives, local(): total_square = lax.psum(local_square, ('blk', 'sub'))  109 us
    psum x1, blocking collectives, local(): grad_one, gb_one = lax.psum((grad_one, gb_one), ('blk', 'sub'))  99.6 us
    ppermute x16, starting transfers between devices, padded_2(): after = lax.ppermute(initial, axis, down)  89.2 us
    ppermute x16, starting transfers between devices, padded_2(): before = lax.ppermute(last, axis, up)  41.6 us
    ppermute x16, waiting for transfers between devices, padded_2(): after = lax.ppermute(initial, axis, down)  27 us
  transfers between devices with their start and end apart: 33, of which 15 were waited for; matrix products, arithmetic and copies ran while one was open for 1% of the time, Pallas kernels for 0%

commit v1 on v0

--- a/solution.py
+++ b/solution.py
@@ -115,7 +115,7 @@
     grad_three, gb_three, delta_three = next_terms(delta_four, weight_four, layer_three, layer_two)
     grad_three, gb_three = lax.psum((grad_three, gb_three), ("blk", "sub"))
     grad_two, gb_two, delta_two = next_terms(delta_three, weight_three, layer_two, layer_one)
-    grad_two, gb_two = lax.psum((grad_two, gb_two), ("blk", "sub"))
+    grad_two, gb_two = lax.psum(lax.psum((grad_two, gb_two), "blk"), "sub")
     grad_one, gb_one, delta_one = next_terms(delta_two, weight_two, layer_one, inputs)
     grad_one, gb_one = lax.psum((grad_one, gb_one), ("blk", "sub"))
     results = (

time: 796 us -> 1330 us (1.67)
  waiting for transfers between devices: 381 us -> 754 us
  blocking collectives: 208 us -> 359 us
    psum x1 -> x3, waiting for transfers between devices: 347 us -> 720 us  [the longest x2 518 us: local(): grad_two, gb_two = lax.psum(lax.psum((grad_two, gb_two), 'blk'), 'sub')]
    psum x0 -> x2, blocking collectives: none -> 146 us  [local(): grad_two, gb_two = lax.psum(lax.psum((grad_two, gb_two), 'blk'), 'sub')]
  transfers between devices with their start and end apart: 33 -> 35, of which waited for: 15 -> 17; matrix products, arithmetic and copies ran while one was open for 1% -> 1% of each run, Pallas kernels for 0% -> 0%
where the time goes in v1:
time: 1330 us; the launch traced here: 1320 us
  waiting for transfers between devices  754 us (57%)
  blocking collectives  359 us (27%)
  starting transfers between devices  131 us (10%)
  matrix products  41.5 us (3%)
  between operations  15.5 us (1%)
    psum x2, waiting for transfers between devices, local(): grad_two, gb_two = lax.psum(lax.psum((grad_two, gb_two), 'blk'), 'sub')  518 us
    psum x1, waiting for transfers between devices, local(): grad_three, gb_three = lax.psum((grad_three, gb_three), ('blk', 'sub'))  202 us
    psum x2, blocking collectives, local(): grad_two, gb_two = lax.psum(lax.psum((grad_two, gb_two), 'blk'), 'sub')  146 us
    psum x1, blocking collectives, local(): total_square = lax.psum(local_square, ('blk', 'sub'))  109 us
    psum x1, blocking collectives, local(): grad_one, gb_one = lax.psum((grad_one, gb_one), ('blk', 'sub'))  104 us
    ppermute x16, starting transfers between devices, padded_2(): after = lax.ppermute(initial, axis, down)  89.2 us
    ppermute x16, starting transfers between devices, padded_2(): before = lax.ppermute(last, axis, up)  41.6 us
    ppermute x16, waiting for transfers between devices, padded_2(): after = lax.ppermute(initial, axis, down)  27 us
  transfers between devices with their start and end apart: 35, of which 17 were waited for; matrix products, arithmetic and copies ran while one was open for 1% of the time, Pallas kernels for 0%

profile of v1, /device:TPU:1, one launch (start us, length us, event | category | flops | bytes accessed | tf_op | source)
XLA Modules:
  0.0 1316.4 jit_solution(11362443287752554139)
XLA Ops:
  7.3 8.9 collective-permute-start.1
  16.2 1.9 collective-permute-start
  18.1 6.8 collective-permute-done
  25.0 2.2 collective-permute-start.2
  29.4 3.0 collective-permute-done.3
  34.6 1.9 collective-permute-start.4
  36.6 9.9 collective-permute-start.5
  47.5 4.5 collective-permute-start.6
  53.4 3.1 collective-permute-done.7
  56.8 1.9 collective-permute-start.8
  58.8 10.0 collective-permute-start.9
  69.8 2.7 collective-permute-start.10
  73.7 3.3 collective-permute-done.11
  77.4 1.9 collective-permute-start.12
  79.4 9.7 collective-permute-start.13
  90.1 4.5 collective-permute-start.14
  95.9 3.1 collective-permute-done.15
  99.4 1.9 collective-permute-start.16
  101.3 10.0 collective-permute-start.17
  112.3 2.7 collective-permute-start.18
  116.3 3.2 collective-permute-done.19
  119.8 1.9 collective-permute-start.20
  121.8 10.0 collective-permute-start.21
  132.8 4.2 collective-permute-start.22
  138.3 3.1 collective-permute-done.23
  141.8 1.9 collective-permute-start.24
  143.7 10.0 collective-permute-start.25
  154.7 2.8 collective-permute-start.26
  159.1 2.8 collective-permute-done.27
  162.3 1.9 collective-permute-start.28
  164.2 10.0 collective-permute-start.29
  176.2 2.5 collective-permute-start.30
  180.7 3.4 fusion.4
  185.5 3.2 fusion.3
  188.7 108.6 %psum.84 = f32[]{:T(128)} all-reduce(f32[]{:T(128)} %multiply_reduce_fusion.9), channel_id=1, replica_groups=mesh['blk'=64,'sub'=8] {'blk','sub'}, use_global_device_ids=true, to_apply=%region_10.0 | all-reduce | flops 1 | bytes 8 | tf_op jit(solution)/shard_map/psum | solution.py:108
  298.6 4.2 fusion.6
  302.8 3.1 fusion.7
  305.9 3.6 fusion.90
  310.9 4.4 fusion.94
  315.3 4.3 fusion.91
  320.9 4.2 fusion.93
  325.1 4.5 fusion.89
  333.3 441.7 %all-reduce.8.cloned.1.call-done = f32[128,128]{1,0:T(8,128)} async-done(((f32[128,128]{1,0:T(8,128)}), f32[128,128]{1,0:T(8,128)}) %all-reduce.8.cloned.1.call-update) | async-done | bytes 65552 | tf_op jit(solution)/shard_map/psum | solution.py:118
  776.7 130.9 %psum.89 = f32[128]{0:T(128)S(1)} all-reduce(f32[128]{0:T(128)S(1)} %get-tuple-element.61), channel_id=1, replica_groups=mesh['blk'=64,'sub'=8] {'blk'}, use_global_device_ids=true, to_apply=%region_17.0 | all-reduce | flops 128 | bytes 1024 | tf_op jit(solution)/shard_map/psum | solution.py:118
  907.7 15.4 %psum.90 = f32[128]{0:T(128)} all-reduce(f32[128]{0:T(128)S(1)} %psum.89), channel_id=1, replica_groups=mesh['blk'=64,'sub'=8] {'sub'}, use_global_device_ids=true, to_apply=%region_18.0 | all-reduce | flops 128 | bytes 1024 | tf_op jit(solution)/shard_map/psum | solution.py:118
  923.1 104.2 %all-reduce.2 = (f32[128,12]{0,1:T(8,128)}, f32[128]{0:T(128)}, f32[128]{0:T(128)}, f32[128]{0:T(128)}, f32[128]{0:T(128)}) all-reduce(f32[128,12]{0,1:T(8,128)S(1)} %fusion.92, f32[128]{0:T(128)S(1)} %get-tuple-element.55, f32[128]{0:T(128)S(1)} %get-tuple-element.57, ...), channel_id=1, replica_groups=mesh['blk'=64,'sub'=8] {'blk','sub'}, use_global_device_ids=true, to_apply=%region_11.0 | all-reduce | flops 2048 | bytes 16384 | tf_op jit(solution)/shard_map/psum | solution.py:120
  1027.3 202.0 %all-reduce.12.cloned.1.call-done = (f32[128,128]{1,0:T(8,128)}, f32[128,128]{1,0:T(8,128)}) async-done(((f32[128,128]{1,0:T(8,128)}, f32[128,128]{1,0:T(8,128)}), (f32[128,128]{1,0:T(8,128)}, f32[128,128]{1,0:T(8,128)})) %all-reduce.12.cloned.1.call-update) | async-done | bytes 131088 | tf_op jit(solution)/shard_map/psum | solution.py:116
  1229.3 75.9 %all-reduce.10.cloned.1.call-done = f32[128,128]{1,0:T(8,128)} async-done(((f32[128,128]{1,0:T(8,128)}), f32[128,128]{1,0:T(8,128)}) %all-reduce.10.cloned.1.call-update) | async-done | bytes 65552 | tf_op jit(solution)/shard_map/psum | solution.py:118
  (127 shorter events, 39.0 us)
Async XLA Ops:
  7.2 291.4 %copy-start = (f32[128,128]{1,0:T(8,128)S(1)}, f32[128,128]{1,0:T(8,128)}, u32[]{:S(2)}) copy-start(f32[128,128]{1,0:T(8,128)} %param.25) | copy-start | bytes 196612
  7.2 49.3 %copy-start.9 = (f32[6,32,128]{2,1,0:T(8,128)S(1)}, f32[6,32,128]{2,1,0:T(8,128)}, u32[]{:S(2)}) copy-start(f32[6,32,128]{2,1,0:T(8,128)} %param.17) | copy-start | bytes 294916
  7.2 49.5 %copy-start.1 = (f32[6,6,32,128]{3,2,1,0:T(8,128)S(1)}, f32[6,6,32,128]{3,2,1,0:T(8,128)}, u32[]{:S(2)}) copy-start(f32[6,6,32,128]{3,2,1,0:T(8,128)} %param.15) | copy-start | bytes 1769476
  7.2 767.8 %all-reduce.8.cloned.1.call-start = ((), (), s32[]{:S(2)}) async-start(), calls=%async_computation | async-start | bytes 131072 | tf_op jit(solution)/shard_map/psum | solution.py:118
  7.3 10.9 collective-permute-start.1
  16.2 8.7 collective-permute-start
  25.0 4.3 collective-permute-start.2
  27.3 5.1 collective-permute-start.3
  34.6 11.8 collective-permute-start.4
  36.6 10.8 collective-permute-start.5
  47.5 5.8 collective-permute-start.6
  52.1 4.4 collective-permute-start.7
  56.8 11.9 collective-permute-start.8
  58.8 10.9 collective-permute-start.9
  69.8 4.0 collective-permute-start.10
  72.4 4.7 collective-permute-start.11
  77.4 11.6 collective-permute-start.12
  79.4 10.6 collective-permute-start.13
  90.1 5.8 collective-permute-start.14
  94.6 4.4 collective-permute-start.15
  99.4 11.9 collective-permute-start.16
  101.3 10.9 collective-permute-start.17
  112.3 46.6 %copy-start.13 = (f32[12,32,128]{2,1,0:T(8,128)S(1)}, f32[12,32,128]{2,1,0:T(8,128)}, u32[]{:S(2)}) copy-start(f32[12,32,128]{2,1,0:T(8,128)} %param.14) | copy-start | bytes 589828
  112.3 4.0 collective-permute-start.18
  115.0 4.5 collective-permute-start.19
  119.8 11.9 collective-permute-start.20
  121.8 10.9 collective-permute-start.21
  132.8 5.5 collective-permute-start.22
  137.0 4.4 collective-permute-start.23
  141.6 32.6 %copy-start.15 = (f32[128,12]{0,1:T(8,128)S(1)}, f32[128,12]{0,1:T(8,128)}, u32[]{:S(2)}) copy-start(f32[128,12]{0,1:T(8,128)} %param.19) | copy-start | bytes 18436
  141.6 32.6 %copy-start.20 = (f32[128]{0:T(128)S(1)}, f32[128]{0:T(128)}, u32[]{:S(2)}) copy-start(f32[128]{0:T(128)} %param.20) | copy-start | bytes 1540
  141.8 11.9 collective-permute-start.24
  143.7 10.9 collective-permute-start.25
  154.7 4.4 collective-permute-start.26
  157.6 4.4 collective-permute-start.27
  159.1 21.7 %copy-start.12 = (f32[128,128]{1,0:T(8,128)S(1)}, f32[128,128]{1,0:T(8,128)}, u32[]{:S(2)}) copy-start(f32[128,128]{1,0:T(8,128)} %param.21) | copy-start | bytes 196612
  159.1 21.7 %copy-start.17 = (f32[128]{0:T(128)S(1)}, f32[128]{0:T(128)}, u32[]{:S(2)}) copy-start(f32[128]{0:T(128)} %param.22) | copy-start | bytes 1540
  162.3 13.8 %collective-permute-start.28 = (f32[6,32,1]{2,1,0:T(8,128)S(1)}, f32[6,32,1]{2,1,0:T(8,128)S(1)}, u32[]{:S(2)}, u32[]{:S(2)}) collective-permute-start(f32[6,32,1]{2,1,0:T(8,128)S(1)} %get-tuple-element.37), channel_id=1, source_target_pairs={{0,8},{8,16},{16,24},{24,32},{32,40},{40,48},{48,56},{56,64},{64,7... | collective-permute-start | bytes 2312 | tf_op jit(solution)/shard_map/ppermute | solution.py:18
  164.2 11.9 collective-permute-start.29
  176.1 8.1 copy-start.2
  176.2 8.0 collective-permute-start.30
  178.8 6.7 copy-start.11
  178.8 6.7 copy-start.18
  178.8 5.4 collective-permute-start.31
  185.5 113.1 %copy-start.16 = (f32[128]{0:T(128)S(1)}, f32[128]{0:T(128)}, u32[]{:S(2)}) copy-start(f32[128]{0:T(128)} %param.27) | copy-start | bytes 1540
  185.5 113.1 %copy-start.19 = (f32[128]{0:T(128)S(1)}, f32[128]{0:T(128)}, u32[]{:S(2)}) copy-start(f32[128]{0:T(128)} %param.26) | copy-start | bytes 1540
  331.4 897.9 %all-reduce.12.cloned.1.call-start = ((), (), s32[]{:S(2)}) async-start(), calls=%async_computation.2 | async-start | bytes 262144 | tf_op jit(solution)/shard_map/psum | solution.py:116
  332.7 972.6 %all-reduce.10.cloned.1.call-start = ((), (), s32[]{:S(2)}) async-start(), calls=%async_computation.1 | async-start | bytes 131072 | tf_op jit(solution)/shard_map/psum | solution.py:118
  (8 other events, 28.6 us)
Sparse Core Ops, SparseCore 0:
  331.5 443.4 all-reduce.7
  782.0 447.2 all-reduce.11
  1232.2 72.9 all-reduce.9
